TPU v7x, 32 devices: a whole 2x2x4 slice. The times are simulated.
32 devices in a mesh: grp: 2 (over x), row: 16 (over z, y, core).
Axes of the slice: x: 2, y: 2, z: 4, core: 2. Of those that a mesh axis runs over, the one named last changes fastest.
Arguments:
- s1_embed: bfloat16 [16384, 768], P(('grp', 'row')), parts along dimension 0, may hold values from -40 to 40
- s2_embed: bfloat16 [16384, 768], P(('grp', 'row')), parts along dimension 0, may hold values from -40 to 40
- block_list: int32 [128, 4], P('grp'), parts along dimension 0, may hold values from 0 to 63, as said below
- footprint: int32 [16384], P('grp'), parts along dimension 0, may hold values from 0 to 2729, never falling along the last dimension, each value on 1 to 4 neighbouring positions
Outputs:
- grad_s1: float32 [16384, 768], P(('grp', 'row')), parts along dimension 0
- grad_s2: float32 [16384, 768], P(('grp', 'row')), parts along dimension 0
There are 2 independent parts, one for each index of `grp`. A program takes and returns all parts, laid end to end along the dimension named above; each array names one. Nothing has to cross between parts.
Inputs may be any that keep to these rules, and one draw needn't show every extreme that they name: Row r of block_list holds 4 distinct column blocks, the first being r itself; for every listed column block c, c // 4 differs from r // 4 by at most 3, counted cyclically over the devices of the row axis.
All inputs are finite; a program needn't handle non-finite values.
Results may differ from a plain program's by a relative error of at most 0.0016.
Values may be sent and summed in bfloat16 or wider, within the bound.
A program may use at most 128 MiB of HBM per device.

v0:
```python
import jax
import jax.numpy as jnp
from jax import lax
from jax.sharding import PartitionSpec as P

BLK = 128
HALF = 3


NEGATIVE = -1e30


def passed_along(array, axis, by):
    count = lax.axis_size(axis)
    return lax.ppermute(array, axis, [(i, (i + by) % count) for i in range(count)])


def combine_stats(top_one, total_one, top_two, total_two):
    highest = jnp.maximum(top_one, top_two)
    return (
        highest,
        total_one * jnp.exp(top_one - highest) + total_two * jnp.exp(top_two - highest),
    )


def pair_scores(row_embed, column_embed):
    return lax.dot_general(
        row_embed, column_embed, (((1,), (1,)), ((), ())), preferred_element_type=jnp.float32
    )


def slot_mask(block_list, footprint, row_device, column_device, rows):
    blocks_here = rows // BLK
    listed = lax.dynamic_slice(
        block_list, (row_device * blocks_here, 0), (blocks_here, block_list.shape[1])
    )
    target = column_device * blocks_here + jnp.arange(blocks_here, dtype=jnp.int32)
    active = jnp.any(listed[:, :, None] == target[None, None, :], axis=1)
    spread = jnp.repeat(jnp.repeat(active, BLK, axis=0), BLK, axis=1)
    foot_rows = lax.dynamic_slice_in_dim(footprint, row_device * rows, rows)
    foot_columns = lax.dynamic_slice_in_dim(footprint, column_device * rows, rows)
    diagonal = jnp.logical_and(row_device == column_device, jnp.eye(rows, dtype=jnp.bool_))
    valid = spread & ((foot_rows[:, None] != foot_columns[None, :]) | diagonal)
    return (valid, diagonal, jnp.any(active))


def slot_stats(row_embed, column_embed, valid, busy):
    rows = row_embed.shape[0]

    def work(operand):
        masked = jnp.where(valid, pair_scores(row_embed, column_embed), NEGATIVE)
        row_top = jnp.max(masked, axis=1)
        row_total = jnp.sum(jnp.where(valid, jnp.exp(masked - row_top[:, None]), 0.0), axis=1)
        column_top = jnp.max(masked, axis=0)
        column_total = jnp.sum(jnp.where(valid, jnp.exp(masked - column_top[None, :]), 0.0), axis=0)
        return (row_top, row_total, column_top, column_total)

    def empty_case(operand):
        lowest = jnp.full((rows,), NEGATIVE, jnp.float32)
        nothing = jnp.zeros((rows,), jnp.float32)
        return (lowest, nothing, lowest, nothing)

    return lax.cond(busy, work, empty_case, 0)


def slot_grads(row_embed, column_embed, valid, diagonal, busy, level_rows, level_columns):
    rows, width = row_embed.shape

    def work(operand):
        masked = jnp.where(valid, pair_scores(row_embed, column_embed), NEGATIVE)
        p_row = jnp.where(valid, jnp.exp(masked - level_rows[:, None]), 0.0)
        p_column = jnp.where(valid, jnp.exp(masked - level_columns[None, :]), 0.0)
        weights = (0.5 * (p_row + p_column) - jnp.where(diagonal, 1.0, 0.0)).astype(jnp.bfloat16)
        to_rows = jnp.dot(weights, column_embed, preferred_element_type=jnp.float32)
        to_columns = lax.dot_general(
            weights, row_embed, (((0,), (0,)), ((), ())), preferred_element_type=jnp.float32
        )
        return (to_rows, to_columns)

    def empty_case(operand):
        zeros = jnp.zeros((rows, width), jnp.float32)
        return (zeros, zeros)

    return lax.cond(busy, work, empty_case, 0)


def shards(s1_embed, s2_embed, block_list, footprint):
    rows, width = s1_embed.shape
    devices = lax.axis_size("row")
    position = lax.axis_index("row")
    offsets = list(range(-HALF, HALF + 1))
    remote = [offset for offset in offsets if offset != 0]

    def neighbour(offset):
        return (position + offset + devices) % devices

    row_masks = {
        offset: slot_mask(block_list, footprint, position, neighbour(offset), rows)
        for offset in offsets
    }
    row_top = jnp.full((rows,), NEGATIVE, jnp.float32)
    row_total = jnp.zeros((rows,), jnp.float32)
    grad_s1 = jnp.zeros((rows, width), jnp.float32)
    grad_s2 = jnp.zeros((rows, width), jnp.float32)
    window = {0: s2_embed}
    for offset in remote:
        window[offset] = passed_along(s2_embed, "row", -offset)
    partial_value = {}
    for offset in offsets:
        valid, diagonal, busy = row_masks[offset]
        top, total, part_top, part_total = slot_stats(s1_embed, window[offset], valid, busy)
        row_top, row_total = combine_stats(row_top, row_total, top, total)
        partial_value[offset] = (part_top, part_total)
    column_top, column_total = partial_value[0]
    for offset in remote:
        got_top, got_total = passed_along(
            (partial_value[offset][0], partial_value[offset][1]), "row", offset
        )
        column_top, column_total = combine_stats(column_top, column_total, got_top, got_total)
    row_level = row_top + jnp.log(row_total)
    column_level = column_top + jnp.log(column_total)
    levels = {0: column_level}
    for offset in remote:
        levels[offset] = passed_along(column_level, "row", -offset)
    for offset in offsets:
        valid, diagonal, busy = row_masks[offset]
        to_rows, to_columns = slot_grads(
            s1_embed, window[offset], valid, diagonal, busy, row_level, levels[offset]
        )
        grad_s1 = grad_s1 + to_rows
        if offset == 0:
            grad_s2 = grad_s2 + to_columns
        else:
            grad_s2 = grad_s2 + passed_along(to_columns, "row", offset)
    return (grad_s1, grad_s2)


def solution(mesh):
    placed = (P(("grp", "row"), None), P(("grp", "row"), None), P("grp", None), P("grp"))
    return jax.shard_map(
        shards,
        mesh=mesh,
        in_specs=placed,
        out_specs=(P(("grp", "row"), None), P(("grp", "row"), None)),
        check_vma=False,
    )
```

profile of v0, /device:TPU:1, one launch (start us, length us, event | category | flops | bytes accessed | tf_op | source)
XLA Modules:
  0.0 283.4 jit_solution(1766638829773139291)
XLA Ops:
  0.6 5.2 %collective-permute-start.4 = (bf16[512,768]{1,0:T(8,128)(2,1)}, bf16[512,768]{1,0:T(8,128)(2,1)S(1)}, u32[]{:S(2)}, u32[]{:S(2)}) collective-permute-start(bf16[512,768]{1,0:T(8,128)(2,1)} %param.33), channel_id=1, source_target_pairs={{0,14},{1,15},{2,0},{3,1},{4,2},{5,3},{6,4},{7,5},{8,6},{9,7},{10,... | collective-permute-start | bytes 2359304 | tf_op jit(solution)/shard_map/ppermute | solution.py:15
  9.3 44.7 %collective-permute-done.4 = bf16[512,768]{1,0:T(8,128)(2,1)S(1)} collective-permute-done((bf16[512,768]{1,0:T(8,128)(2,1)}, bf16[512,768]{1,0:T(8,128)(2,1)S(1)}, u32[]{:S(2)}, u32[]{:S(2)}) %collective-permute-start.4) | collective-permute-done | bytes 786464 | tf_op jit(solution)/shard_map/ppermute | solution.py:15
  54.0 3.7 %collective-permute-start.5 = (bf16[512,768]{1,0:T(8,128)(2,1)}, bf16[512,768]{1,0:T(8,128)(2,1)}, u32[]{:S(2)}, u32[]{:S(2)}) collective-permute-start(bf16[512,768]{1,0:T(8,128)(2,1)} %param.33), channel_id=1, source_target_pairs={{0,13},{1,14},{2,15},{3,0},{4,1},{5,2},{6,3},{7,4},{8,5},{9,6},{10... | collective-permute-start | bytes 2359304 | tf_op jit(solution)/shard_map/ppermute | solution.py:15
  70.6 2.6 conditional.19
  75.2 3.7 %conditional.18 = (f32[512]{0:T(512)}, f32[512]{0:T(512)S(1)}, f32[512]{0:T(512)}, f32[512]{0:T(512)S(1)}) conditional(s32[]{:T(128)} %convert_element_type.53, () %tuple.129, (bf16[512,768]{1,0:T(8,128)(2,1)S(1)}, bf16[512,768]{1,0:T(8,128)(2,1)}, pred[512,512]{1,0:T(32,128)(4,1)S(1)}) %tuple.233), branch_computations={%region_34.35_spmd, %region_35.40_spmd} | conditional | flops 405010432 | bytes 4206624 | solution.py:63
  75.3 2.4 fusion.49
  79.0 3.7 %conditional.16 = (f32[512]{0:T(512)}, f32[512]{0:T(512)S(1)}, f32[512]{0:T(512)}, f32[512]{0:T(512)S(1)}) conditional(s32[]{:T(128)} %convert_element_type.51, () %tuple.125, (bf16[512,768]{1,0:T(8,128)(2,1)S(1)}, bf16[512,768]{1,0:T(8,128)(2,1)}, pred[512,512]{1,0:T(32,128)(4,1)S(1)}) %tuple.234), branch_computations={%region_18.19_spmd, %region_19.24_spmd} | conditional | flops 405010432 | bytes 4206624 | solution.py:63
  82.9 3.7 %conditional.15 = (f32[512]{0:T(512)}, f32[512]{0:T(512)S(1)}, f32[512]{0:T(512)}, f32[512]{0:T(512)S(1)}) conditional(s32[]{:T(128)} %convert_element_type.50, () %tuple.123, (bf16[512,768]{1,0:T(8,128)(2,1)S(1)}, bf16[512,768]{1,0:T(8,128)(2,1)}, pred[512,512]{1,0:T(32,128)(4,1)S(1)}) %tuple.235), branch_computations={%region_10.11_spmd, %region_11.16_spmd} | conditional | flops 405010432 | bytes 4206624 | solution.py:63
  87.1 4.2 %collective-permute-start.14 = (f32[512]{0:T(512)S(1)}, f32[512]{0:T(512)S(1)}, u32[]{:S(2)}, u32[]{:S(2)}) collective-permute-start(f32[512]{0:T(512)S(1)} %get-tuple-element.257), channel_id=1, source_target_pairs={{0,15},{1,0},{2,1},{3,2},{4,3},{5,4},{6,5},{7,6},{8,7},{9,8},{10,9... | collective-permute-start | bytes 6152 | tf_op jit(solution)/shard_map/ppermute | solution.py:15
  96.0 3.9 %conditional.14 = (f32[512]{0:T(512)}, f32[512]{0:T(512)S(1)}, f32[512]{0:T(512)}, f32[512]{0:T(512)S(1)}) conditional(s32[]{:T(128)} %convert_element_type.49, () %tuple.121, (bf16[512,768]{1,0:T(8,128)(2,1)S(1)}, bf16[512,768]{1,0:T(8,128)(2,1)}, pred[512,512]{1,0:T(32,128)(4,1)S(1)}) %tuple.236), branch_computations={%region_2.3_spmd, %region_3.8_spmd} | conditional | flops 405010432 | bytes 4206624 | solution.py:63
  96.2 2.4 fusion.45
  99.9 3.7 %conditional.20 = (f32[512]{0:T(512)}, f32[512]{0:T(512)S(1)}, f32[512]{0:T(512)}, f32[512]{0:T(512)S(1)}) conditional(s32[]{:T(128)} %convert_element_type.55, () %tuple.133, (bf16[512,768]{1,0:T(8,128)(2,1)S(1)}, bf16[512,768]{1,0:T(8,128)(2,1)}, pred[512,512]{1,0:T(32,128)(4,1)S(1)}) %tuple.237), branch_computations={%region_50.51_spmd, %region_51.56_spmd} | conditional | flops 405010432 | bytes 4206624 | solution.py:63
  108.5 3.7 %conditional.17 = (f32[512]{0:T(512)}, f32[512]{0:T(512)S(1)}, f32[512]{0:T(512)}, f32[512]{0:T(512)S(1)}) conditional(s32[]{:T(128)} %convert_element_type.52, () %tuple.127, (bf16[512,768]{1,0:T(8,128)(2,1)S(1)}, bf16[512,768]{1,0:T(8,128)(2,1)}, pred[512,512]{1,0:T(32,128)(4,1)S(1)}) %tuple.238), branch_computations={%region_26.27_spmd, %region_27.32_spmd} | conditional | flops 405010432 | bytes 4206624 | solution.py:63
  113.8 4.9 %collective-permute-done.18 = f32[512]{0:T(512)S(1)} collective-permute-done((f32[512]{0:T(512)S(1)}, f32[512]{0:T(512)S(1)}, u32[]{:S(2)}, u32[]{:S(2)}) %collective-permute-start.18) | collective-permute-done | bytes 2080 | tf_op jit(solution)/shard_map/ppermute | solution.py:15
  118.7 5.8 %conditional.21 = (f32[512,768]{1,0:T(8,128)S(1)}, f32[512,768]{1,0:T(8,128)}) conditional(s32[]{:T(128)} %convert_element_type.49, () %tuple.120, (bf16[512,768]{1,0:T(8,128)(2,1)S(1)}, bf16[512,768]{1,0:T(8,128)(2,1)}, pred[512,512]{1,0:T(32,128)(4,1)S(1)}, f32[512]{0:T(512)S(1)}, f32[512]{0:T(512)S(1)}, ...), branch_computations={%region_56.57_spmd, %region_57.58_spmd} | conditional | flops 1210580992 | bytes 8392720 | solution.py:84
  128.3 4.0 %collective-permute-start.23 = (f32[512]{0:T(512)S(1)}, f32[512]{0:T(512)S(1)}, u32[]{:S(2)}, u32[]{:S(2)}) collective-permute-start(f32[512]{0:T(512)S(1)} %log_add_fusion), channel_id=1, source_target_pairs={{0,13},{1,14},{2,15},{3,0},{4,1},{5,2},{6,3},{7,4},{8,5},{9,6},{10... | collective-permute-start | bytes 6152 | tf_op jit(solution)/shard_map/ppermute | solution.py:15
  132.6 10.8 %collective-permute-start.20 = (f32[512]{0:T(512)S(1)}, f32[512]{0:T(512)S(1)}, u32[]{:S(2)}, u32[]{:S(2)}) collective-permute-start(f32[512]{0:T(512)S(1)} %log_add_fusion), channel_id=1, source_target_pairs={{0,1},{1,2},{2,3},{3,4},{4,5},{5,6},{6,7},{7,8},{8,9},{9,10},{10,1... | collective-permute-start | bytes 6152 | tf_op jit(solution)/shard_map/ppermute | solution.py:15
  143.5 6.0 %conditional.22 = (f32[512,768]{1,0:T(8,128)S(1)}, f32[512,768]{1,0:T(8,128)}) conditional(s32[]{:T(128)} %convert_element_type.50, () %tuple.136, (bf16[512,768]{1,0:T(8,128)(2,1)S(1)}, bf16[512,768]{1,0:T(8,128)(2,1)}, pred[512,512]{1,0:T(32,128)(4,1)}, f32[512]{0:T(512)S(1)}, f32[512]{0:T(512)S(1)}, ...), branch_computations={%region_58.59_spmd, %region_59.60_spmd} | conditional | flops 1210580992 | bytes 8392720 | solution.py:84
  143.5 2.5 subtract_convert_fusion.1
  149.5 4.6 %collective-permute-start.25 = (f32[512,768]{1,0:T(8,128)}, f32[512,768]{1,0:T(8,128)}, u32[]{:S(2)}, u32[]{:S(2)}) collective-permute-start(f32[512,768]{1,0:T(8,128)} %get-tuple-element.269), channel_id=1, source_target_pairs={{0,14},{1,15},{2,0},{3,1},{4,2},{5,3},{6,4},{7,5},{8,6},{9,7},{10,... | collective-permute-start | bytes 4718600 | tf_op jit(solution)/shard_map/ppermute | solution.py:15
  154.1 6.1 %conditional.23 = (f32[512,768]{1,0:T(8,128)S(1)}, f32[512,768]{1,0:T(8,128)}) conditional(s32[]{:T(128)} %convert_element_type.51, () %tuple.138, (bf16[512,768]{1,0:T(8,128)(2,1)S(1)}, bf16[512,768]{1,0:T(8,128)(2,1)}, pred[512,512]{1,0:T(32,128)(4,1)}, f32[512]{0:T(512)S(1)}, f32[512]{0:T(512)S(1)}, ...), branch_computations={%region_60.61_spmd, %region_61.62_spmd} | conditional | flops 1210580992 | bytes 8392720 | solution.py:84
  154.1 2.6 subtract_convert_fusion.2
  161.4 5.8 %conditional.25 = (f32[512,768]{1,0:T(8,128)S(1)}, f32[512,768]{1,0:T(8,128)}) conditional(s32[]{:T(128)} %convert_element_type.53, () %tuple.142, (bf16[512,768]{1,0:T(8,128)(2,1)S(1)}, bf16[512,768]{1,0:T(8,128)(2,1)}, pred[512,512]{1,0:T(32,128)(4,1)S(1)}, f32[512]{0:T(512)S(1)}, f32[512]{0:T(512)S(1)}, ...), branch_computations={%region_64.65_spmd, %region_65.66_spmd} | conditional | flops 1210580992 | bytes 8392720 | solution.py:84
  168.3 4.7 %conditional.26 = (f32[512,768]{1,0:T(8,128)S(1)}, f32[512,768]{1,0:T(8,128)}) conditional(s32[]{:T(128)} %convert_element_type.54, () %tuple.144, (bf16[512,768]{1,0:T(8,128)(2,1)S(1)}, bf16[512,768]{1,0:T(8,128)(2,1)}, pred[512,512]{1,0:T(32,128)(4,1)S(1)}, f32[512]{0:T(512)S(1)}, f32[512]{0:T(512)S(1)}, ...), branch_computations={%region_66.67_spmd, %region_67.68_spmd} | conditional | flops 1210580992 | bytes 11538476 | solution.py:84
  172.9 3.2 %collective-permute-start.28 = (f32[512,768]{1,0:T(8,128)}, f32[512,768]{1,0:T(8,128)}, u32[]{:S(2)}, u32[]{:S(2)}) collective-permute-start(f32[512,768]{1,0:T(8,128)} %get-tuple-element.273), channel_id=1, source_target_pairs={{0,2},{1,3},{2,4},{3,5},{4,6},{5,7},{6,8},{7,9},{8,10},{9,11},{10,... | collective-permute-start | bytes 4718600 | tf_op jit(solution)/shard_map/ppermute | solution.py:15
  176.1 5.6 %conditional.27 = (f32[512,768]{1,0:T(8,128)S(1)}, f32[512,768]{1,0:T(8,128)}) conditional(s32[]{:T(128)} %convert_element_type.55, () %tuple.146, (bf16[512,768]{1,0:T(8,128)(2,1)S(1)}, bf16[512,768]{1,0:T(8,128)(2,1)}, pred[512,512]{1,0:T(32,128)(4,1)S(1)}, f32[512]{0:T(512)S(1)}, f32[512]{0:T(512)S(1)}, ...), branch_computations={%region_68.69_spmd, %region_69.70_spmd} | conditional | flops 1210580992 | bytes 8392720 | solution.py:84
  182.9 5.7 %conditional.24 = (f32[512,768]{1,0:T(8,128)}, f32[512,768]{1,0:T(8,128)}) conditional(s32[]{:T(128)} %convert_element_type.52, () %tuple.140, (bf16[512,768]{1,0:T(8,128)(2,1)S(1)}, bf16[512,768]{1,0:T(8,128)(2,1)}, pred[512,512]{1,0:T(32,128)(4,1)S(1)}, f32[512]{0:T(512)S(1)}, f32[512]{0:T(512)S(1)}, ...), branch_computations={%region_62.63_spmd, %region_63.64_spmd} | conditional | flops 1210580992 | bytes 11538476 | solution.py:84
  188.6 5.7 %add_add_fusion.1 = f32[512,768]{1,0:T(8,128)} fusion(f32[512,768]{1,0:T(8,128)} %copy-done.6, f32[512,768]{1,0:T(8,128)} %copy-done.5, f32[512,768]{1,0:T(8,128)} %copy-done.4, f32[512,768]{1,0:T(8,128)} %get-tuple-element.264, f32[512,768]{1,0:T(8,128)} %copy-done.3, f32[512,768]{1,0:T(8,128)S(1)} %get-tuple-element.261, f32[512,768]{1,0:T(8,128)} %copy-done.2), kind=kLoop, calls=%fused_computation.36 | loop fusion | flops 2359296 | bytes 12582912 | tf_op jit(solution)/shard_map/add | solution.py:130
  194.3 60.6 %collective-permute-done.25 = f32[512,768]{1,0:T(8,128)} collective-permute-done((f32[512,768]{1,0:T(8,128)}, f32[512,768]{1,0:T(8,128)}, u32[]{:S(2)}, u32[]{:S(2)}) %collective-permute-start.25) | collective-permute-done | bytes 1572896 | tf_op jit(solution)/shard_map/ppermute | solution.py:15
  254.9 16.4 %collective-permute-done.26 = f32[512,768]{1,0:T(8,128)} collective-permute-done((f32[512,768]{1,0:T(8,128)}, f32[512,768]{1,0:T(8,128)}, u32[]{:S(2)}, u32[]{:S(2)}) %collective-permute-start.26) | collective-permute-done | bytes 1572896 | tf_op jit(solution)/shard_map/ppermute | solution.py:15
  271.2 6.2 %collective-permute-done.28 = f32[512,768]{1,0:T(8,128)} collective-permute-done((f32[512,768]{1,0:T(8,128)}, f32[512,768]{1,0:T(8,128)}, u32[]{:S(2)}, u32[]{:S(2)}) %collective-permute-start.28) | collective-permute-done | bytes 1572896 | tf_op jit(solution)/shard_map/ppermute | solution.py:15
  277.4 6.0 %add_add_fusion = f32[512,768]{1,0:T(8,128)} fusion(f32[512,768]{1,0:T(8,128)} %collective-permute-done.29, f32[512,768]{1,0:T(8,128)} %collective-permute-done.28, f32[512,768]{1,0:T(8,128)} %collective-permute-done.27, f32[512,768]{1,0:T(8,128)} %get-tuple-element.271, f32[512,768]{1,0:T(8,128)} %collective-permute-done.26, ...), kind=kLoop, calls=%fused_computation.35 | loop fusion | flops 2359296 | bytes 12582912 | tf_op jit(solution)/shard_map/add | solution.py:134
  (140 shorter events, 87.6 us)
Async XLA Ops:
  0.6 53.3 %collective-permute-start.4 = (bf16[512,768]{1,0:T(8,128)(2,1)}, bf16[512,768]{1,0:T(8,128)(2,1)S(1)}, u32[]{:S(2)}, u32[]{:S(2)}) collective-permute-start(bf16[512,768]{1,0:T(8,128)(2,1)} %param.33), channel_id=1, source_target_pairs={{0,14},{1,15},{2,0},{3,1},{4,2},{5,3},{6,4},{7,5},{8,6},{9,7},{10,... | collective-permute-start | bytes 2359304 | tf_op jit(solution)/shard_map/ppermute | solution.py:15
  5.8 67.4 %collective-permute-start.3 = (bf16[512,768]{1,0:T(8,128)(2,1)}, bf16[512,768]{1,0:T(8,128)(2,1)}, u32[]{:S(2)}, u32[]{:S(2)}) collective-permute-start(bf16[512,768]{1,0:T(8,128)(2,1)} %param.33), channel_id=1, source_target_pairs={{0,15},{1,0},{2,1},{3,2},{4,3},{5,4},{6,5},{7,6},{8,7},{9,8},{10,9... | collective-permute-start | bytes 2359304 | tf_op jit(solution)/shard_map/ppermute | solution.py:15
  6.8 66.5 %collective-permute-start.2 = (bf16[512,768]{1,0:T(8,128)(2,1)}, bf16[512,768]{1,0:T(8,128)(2,1)}, u32[]{:S(2)}, u32[]{:S(2)}) collective-permute-start(bf16[512,768]{1,0:T(8,128)(2,1)} %param.33), channel_id=1, source_target_pairs={{0,1},{1,2},{2,3},{3,4},{4,5},{5,6},{6,7},{7,8},{8,9},{9,10},{10,1... | collective-permute-start | bytes 2359304 | tf_op jit(solution)/shard_map/ppermute | solution.py:15
  7.6 75.1 %collective-permute-start.1 = (bf16[512,768]{1,0:T(8,128)(2,1)}, bf16[512,768]{1,0:T(8,128)(2,1)}, u32[]{:S(2)}, u32[]{:S(2)}) collective-permute-start(bf16[512,768]{1,0:T(8,128)(2,1)} %param.33), channel_id=1, source_target_pairs={{0,2},{1,3},{2,4},{3,5},{4,6},{5,7},{6,8},{7,9},{8,10},{9,11},{10,... | collective-permute-start | bytes 2359304 | tf_op jit(solution)/shard_map/ppermute | solution.py:15
  7.6 79.0 %collective-permute-start = (bf16[512,768]{1,0:T(8,128)(2,1)}, bf16[512,768]{1,0:T(8,128)(2,1)}, u32[]{:S(2)}, u32[]{:S(2)}) collective-permute-start(bf16[512,768]{1,0:T(8,128)(2,1)} %param.33), channel_id=1, source_target_pairs={{0,3},{1,4},{2,5},{3,6},{4,7},{5,8},{6,9},{7,10},{8,11},{9,12},{10... | collective-permute-start | bytes 2359304 | tf_op jit(solution)/shard_map/ppermute | solution.py:15
  54.0 14.4 %copy-start.10 = (bf16[512,768]{1,0:T(8,128)(2,1)}, bf16[512,768]{1,0:T(8,128)(2,1)S(1)}, u32[]{:S(2)}) copy-start(bf16[512,768]{1,0:T(8,128)(2,1)S(1)} %collective-permute-done.4) | copy-start | bytes 2359300
  54.0 32.7 %collective-permute-start.5 = (bf16[512,768]{1,0:T(8,128)(2,1)}, bf16[512,768]{1,0:T(8,128)(2,1)}, u32[]{:S(2)}, u32[]{:S(2)}) collective-permute-start(bf16[512,768]{1,0:T(8,128)(2,1)} %param.33), channel_id=1, source_target_pairs={{0,13},{1,14},{2,15},{3,0},{4,1},{5,2},{6,3},{7,4},{8,5},{9,6},{10... | collective-permute-start | bytes 2359304 | tf_op jit(solution)/shard_map/ppermute | solution.py:15
  70.6 12.3 %copy-start.8 = (pred[512,512]{1,0:T(32,128)(4,1)}, pred[512,512]{1,0:T(32,128)(4,1)S(1)}, u32[]{:S(2)}) copy-start(pred[512,512]{1,0:T(32,128)(4,1)S(1)} %get-tuple-element.344) | copy-start | bytes 786436
  73.2 13.9 %collective-permute-start.10 = (f32[512]{0:T(512)}, f32[512]{0:T(512)S(1)}, u32[]{:S(2)}, u32[]{:S(2)}) collective-permute-start(f32[512]{0:T(512)} %get-tuple-element.252), channel_id=1, source_target_pairs={{0,2},{1,3},{2,4},{3,5},{4,6},{5,7},{6,8},{7,9},{8,10},{9,11},{10,... | collective-permute-start | bytes 6152 | tf_op jit(solution)/shard_map/ppermute | solution.py:15
  73.3 18.1 %collective-permute-start.16 = (f32[512]{0:T(512)S(1)}, f32[512]{0:T(512)S(1)}, u32[]{:S(2)}, u32[]{:S(2)}) collective-permute-start(f32[512]{0:T(512)S(1)} %get-tuple-element.259), channel_id=1, source_target_pairs={{0,2},{1,3},{2,4},{3,5},{4,6},{5,7},{6,8},{7,9},{8,10},{9,11},{10,... | collective-permute-start | bytes 6152 | tf_op jit(solution)/shard_map/ppermute | solution.py:15
  82.7 20.9 %collective-permute-start.9 = (f32[512]{0:T(512)}, f32[512]{0:T(512)S(1)}, u32[]{:S(2)}, u32[]{:S(2)}) collective-permute-start(f32[512]{0:T(512)} %get-tuple-element.251), channel_id=1, source_target_pairs={{0,1},{1,2},{2,3},{3,4},{4,5},{5,6},{6,7},{7,8},{8,9},{9,10},{10,1... | collective-permute-start | bytes 6152 | tf_op jit(solution)/shard_map/ppermute | solution.py:15
  86.6 17.1 %collective-permute-start.15 = (f32[512]{0:T(512)S(1)}, f32[512]{0:T(512)S(1)}, u32[]{:S(2)}, u32[]{:S(2)}) collective-permute-start(f32[512]{0:T(512)S(1)} %get-tuple-element.258), channel_id=1, source_target_pairs={{0,1},{1,2},{2,3},{3,4},{4,5},{5,6},{6,7},{7,8},{8,9},{9,10},{10,1... | collective-permute-start | bytes 6152 | tf_op jit(solution)/shard_map/ppermute | solution.py:15
  86.6 17.4 %collective-permute-start.8 = (f32[512]{0:T(512)}, f32[512]{0:T(512)S(1)}, u32[]{:S(2)}, u32[]{:S(2)}) collective-permute-start(f32[512]{0:T(512)} %get-tuple-element.250), channel_id=1, source_target_pairs={{0,15},{1,0},{2,1},{3,2},{4,3},{5,4},{6,5},{7,6},{8,7},{9,8},{10,9... | collective-permute-start | bytes 6152 | tf_op jit(solution)/shard_map/ppermute | solution.py:15
  87.1 16.9 %collective-permute-start.14 = (f32[512]{0:T(512)S(1)}, f32[512]{0:T(512)S(1)}, u32[]{:S(2)}, u32[]{:S(2)}) collective-permute-start(f32[512]{0:T(512)S(1)} %get-tuple-element.257), channel_id=1, source_target_pairs={{0,15},{1,0},{2,1},{3,2},{4,3},{5,4},{6,5},{7,6},{8,7},{9,8},{10,9... | collective-permute-start | bytes 6152 | tf_op jit(solution)/shard_map/ppermute | solution.py:15
  91.4 14.4 %collective-permute-start.7 = (f32[512]{0:T(512)}, f32[512]{0:T(512)S(1)}, u32[]{:S(2)}, u32[]{:S(2)}) collective-permute-start(f32[512]{0:T(512)} %get-tuple-element.249), channel_id=1, source_target_pairs={{0,14},{1,15},{2,0},{3,1},{4,2},{5,3},{6,4},{7,5},{8,6},{9,7},{10,... | collective-permute-start | bytes 6152 | tf_op jit(solution)/shard_map/ppermute | solution.py:15
  103.6 8.7 %collective-permute-start.13 = (f32[512]{0:T(512)S(1)}, f32[512]{0:T(512)S(1)}, u32[]{:S(2)}, u32[]{:S(2)}) collective-permute-start(f32[512]{0:T(512)S(1)} %get-tuple-element.256), channel_id=1, source_target_pairs={{0,14},{1,15},{2,0},{3,1},{4,2},{5,3},{6,4},{7,5},{8,6},{9,7},{10,... | collective-permute-start | bytes 6152 | tf_op jit(solution)/shard_map/ppermute | solution.py:15
  103.6 8.6 %collective-permute-start.6 = (f32[512]{0:T(512)}, f32[512]{0:T(512)S(1)}, u32[]{:S(2)}, u32[]{:S(2)}) collective-permute-start(f32[512]{0:T(512)} %get-tuple-element.248), channel_id=1, source_target_pairs={{0,13},{1,14},{2,15},{3,0},{4,1},{5,2},{6,3},{7,4},{8,5},{9,6},{10... | collective-permute-start | bytes 6152 | tf_op jit(solution)/shard_map/ppermute | solution.py:15
  104.0 8.2 %collective-permute-start.12 = (f32[512]{0:T(512)S(1)}, f32[512]{0:T(512)S(1)}, u32[]{:S(2)}, u32[]{:S(2)}) collective-permute-start(f32[512]{0:T(512)S(1)} %get-tuple-element.255), channel_id=1, source_target_pairs={{0,13},{1,14},{2,15},{3,0},{4,1},{5,2},{6,3},{7,4},{8,5},{9,6},{10... | collective-permute-start | bytes 6152 | tf_op jit(solution)/shard_map/ppermute | solution.py:15
  104.1 8.2 %collective-permute-start.11 = (f32[512]{0:T(512)}, f32[512]{0:T(512)S(1)}, u32[]{:S(2)}, u32[]{:S(2)}) collective-permute-start(f32[512]{0:T(512)} %get-tuple-element.253), channel_id=1, source_target_pairs={{0,3},{1,4},{2,5},{3,6},{4,7},{5,8},{6,9},{7,10},{8,11},{9,12},{10... | collective-permute-start | bytes 6152 | tf_op jit(solution)/shard_map/ppermute | solution.py:15
  105.8 6.5 %collective-permute-start.17 = (f32[512]{0:T(512)S(1)}, f32[512]{0:T(512)S(1)}, u32[]{:S(2)}, u32[]{:S(2)}) collective-permute-start(f32[512]{0:T(512)S(1)} %get-tuple-element.260), channel_id=1, source_target_pairs={{0,3},{1,4},{2,5},{3,6},{4,7},{5,8},{6,9},{7,10},{8,11},{9,12},{10... | collective-permute-start | bytes 6152 | tf_op jit(solution)/shard_map/ppermute | solution.py:15
  113.0 5.8 %collective-permute-start.18 = (f32[512]{0:T(512)S(1)}, f32[512]{0:T(512)S(1)}, u32[]{:S(2)}, u32[]{:S(2)}) collective-permute-start(f32[512]{0:T(512)S(1)} %log_add_fusion), channel_id=1, source_target_pairs={{0,3},{1,4},{2,5},{3,6},{4,7},{5,8},{6,9},{7,10},{8,11},{9,12},{10... | collective-permute-start | bytes 6152 | tf_op jit(solution)/shard_map/ppermute | solution.py:15
  124.5 57.3 %collective-permute-start.24 = (f32[512,768]{1,0:T(8,128)}, f32[512,768]{1,0:T(8,128)}, u32[]{:S(2)}, u32[]{:S(2)}) collective-permute-start(f32[512,768]{1,0:T(8,128)} %get-tuple-element.268), channel_id=1, source_target_pairs={{0,13},{1,14},{2,15},{3,0},{4,1},{5,2},{6,3},{7,4},{8,5},{9,6},{10... | collective-permute-start | bytes 4718600 | tf_op jit(solution)/shard_map/ppermute | solution.py:15
  127.2 5.4 %collective-permute-start.19 = (f32[512]{0:T(512)S(1)}, f32[512]{0:T(512)S(1)}, u32[]{:S(2)}, u32[]{:S(2)}) collective-permute-start(f32[512]{0:T(512)S(1)} %log_add_fusion), channel_id=1, source_target_pairs={{0,2},{1,3},{2,4},{3,5},{4,6},{5,7},{6,8},{7,9},{8,10},{9,11},{10,... | collective-permute-start | bytes 6152 | tf_op jit(solution)/shard_map/ppermute | solution.py:15
  128.3 44.7 %collective-permute-start.23 = (f32[512]{0:T(512)S(1)}, f32[512]{0:T(512)S(1)}, u32[]{:S(2)}, u32[]{:S(2)}) collective-permute-start(f32[512]{0:T(512)S(1)} %log_add_fusion), channel_id=1, source_target_pairs={{0,13},{1,14},{2,15},{3,0},{4,1},{5,2},{6,3},{7,4},{8,5},{9,6},{10... | collective-permute-start | bytes 6152 | tf_op jit(solution)/shard_map/ppermute | solution.py:15
  132.2 34.9 %collective-permute-start.22 = (f32[512]{0:T(512)S(1)}, f32[512]{0:T(512)S(1)}, u32[]{:S(2)}, u32[]{:S(2)}) collective-permute-start(f32[512]{0:T(512)S(1)} %log_add_fusion), channel_id=1, source_target_pairs={{0,14},{1,15},{2,0},{3,1},{4,2},{5,3},{6,4},{7,5},{8,6},{9,7},{10,... | collective-permute-start | bytes 6152 | tf_op jit(solution)/shard_map/ppermute | solution.py:15
  132.3 28.0 %collective-permute-start.21 = (f32[512]{0:T(512)S(1)}, f32[512]{0:T(512)S(1)}, u32[]{:S(2)}, u32[]{:S(2)}) collective-permute-start(f32[512]{0:T(512)S(1)} %log_add_fusion), channel_id=1, source_target_pairs={{0,15},{1,0},{2,1},{3,2},{4,3},{5,4},{6,5},{7,6},{8,7},{9,8},{10,9... | collective-permute-start | bytes 6152 | tf_op jit(solution)/shard_map/ppermute | solution.py:15
  132.6 16.9 %collective-permute-start.20 = (f32[512]{0:T(512)S(1)}, f32[512]{0:T(512)S(1)}, u32[]{:S(2)}, u32[]{:S(2)}) collective-permute-start(f32[512]{0:T(512)S(1)} %log_add_fusion), channel_id=1, source_target_pairs={{0,1},{1,2},{2,3},{3,4},{4,5},{5,6},{6,7},{7,8},{8,9},{9,10},{10,1... | collective-permute-start | bytes 6152 | tf_op jit(solution)/shard_map/ppermute | solution.py:15
  149.5 105.3 %collective-permute-start.25 = (f32[512,768]{1,0:T(8,128)}, f32[512,768]{1,0:T(8,128)}, u32[]{:S(2)}, u32[]{:S(2)}) collective-permute-start(f32[512,768]{1,0:T(8,128)} %get-tuple-element.269), channel_id=1, source_target_pairs={{0,14},{1,15},{2,0},{3,1},{4,2},{5,3},{6,4},{7,5},{8,6},{9,7},{10,... | collective-permute-start | bytes 4718600 | tf_op jit(solution)/shard_map/ppermute | solution.py:15
  160.2 111.0 %collective-permute-start.26 = (f32[512,768]{1,0:T(8,128)}, f32[512,768]{1,0:T(8,128)}, u32[]{:S(2)}, u32[]{:S(2)}) collective-permute-start(f32[512,768]{1,0:T(8,128)} %get-tuple-element.270), channel_id=1, source_target_pairs={{0,15},{1,0},{2,1},{3,2},{4,3},{5,4},{6,5},{7,6},{8,7},{9,8},{10,9... | collective-permute-start | bytes 4718600 | tf_op jit(solution)/shard_map/ppermute | solution.py:15
  167.1 104.1 %collective-permute-start.27 = (f32[512,768]{1,0:T(8,128)}, f32[512,768]{1,0:T(8,128)}, u32[]{:S(2)}, u32[]{:S(2)}) collective-permute-start(f32[512,768]{1,0:T(8,128)} %get-tuple-element.272), channel_id=1, source_target_pairs={{0,1},{1,2},{2,3},{3,4},{4,5},{5,6},{6,7},{7,8},{8,9},{9,10},{10,1... | collective-permute-start | bytes 4718600 | tf_op jit(solution)/shard_map/ppermute | solution.py:15
  172.9 104.5 %collective-permute-start.28 = (f32[512,768]{1,0:T(8,128)}, f32[512,768]{1,0:T(8,128)}, u32[]{:S(2)}, u32[]{:S(2)}) collective-permute-start(f32[512,768]{1,0:T(8,128)} %get-tuple-element.273), channel_id=1, source_target_pairs={{0,2},{1,3},{2,4},{3,5},{4,6},{5,7},{6,8},{7,9},{8,10},{9,11},{10,... | collective-permute-start | bytes 4718600 | tf_op jit(solution)/shard_map/ppermute | solution.py:15
  181.8 95.6 %collective-permute-start.29 = (f32[512,768]{1,0:T(8,128)}, f32[512,768]{1,0:T(8,128)}, u32[]{:S(2)}, u32[]{:S(2)}) collective-permute-start(f32[512,768]{1,0:T(8,128)} %get-tuple-element.274), channel_id=1, source_target_pairs={{0,3},{1,4},{2,5},{3,6},{4,7},{5,8},{6,9},{7,10},{8,11},{9,12},{10... | collective-permute-start | bytes 4718600 | tf_op jit(solution)/shard_map/ppermute | solution.py:15
  (12 other events, 43.4 us)
where the time goes:
time: 284 us; the launch traced here: 283 us
  waiting for transfers between devices  133 us (47%)
  matrix products  55.4 us (20%)
  starting transfers between devices  45.1 us (16%)
  other arithmetic  29.3 us (10%)
  local copies, waits for them, and re-layouts  15.1 us (5%)
  between operations  5.33 us (2%)
    ppermute x30, waiting for transfers between devices, passed_along(): lax.ppermute(array, axis, [(i, (i + by) % count) for i in range(count)])  133 us
    ppermute x30, starting transfers between devices, passed_along(): lax.ppermute(array, axis, [(i, (i + by) % count) for i in range(count)])  45.1 us
    dot_general x14, matrix products, pair_scores(): lax.dot_general(row_embed, column_embed, (((1,), (1,)), ((), ())), prefer...  32.1 us
    dot_general x7, matrix products, work(): lax.dot_general(weights, row_embed, (((0,), (0,)), ((), ())), preferred_e...  12.4 us
    broadcast_in_dim x14, local copies, waits for them, and re-layouts, slot_mask(): spread = jnp.repeat(jnp.repeat(active, BLK, axis=0), BLK, axis=1)  11.3 us
    dot_general x7, matrix products, work(): to_rows = jnp.dot(weights, column_embed, preferred_element_type=jnp.float32)  10.8 us
    reduce_sum x7, other arithmetic, work(): jnp.sum(jnp.where(valid, jnp.exp(masked - column_top[None, :]), 0.0), axi...  8.7 us
    add x1, other arithmetic, shards(): grad_s2 = grad_s2 + passed_along(to_columns, 'row', offset)  6.01 us
  transfers between devices with their start and end apart: 30, of which 5 were waited for; matrix products, arithmetic and copies ran while one was open for 30% of the time, Pallas kernels for 0%

commit v1 on v0

v1 whole, which is shorter than its diff:
```python
import functools

import jax
import jax.numpy as jnp
from jax import lax
from jax.experimental import pallas as pl
from jax.experimental.pallas import tpu as pltpu
from jax.sharding import PartitionSpec as P

BLK = 128
NEGATIVE = -1e30
ROLES = 6
OWN = 6
MESH = pl.DeviceIdType.MESH


def kernel(
    n, s1, s2, blist, foot, g1, g2,
    win, logit, act, footw, footc, mx, sm, levc, levw,
    send_sem, recv_sem, lev_send, lev_recv,
):
    rows, width = s1.shape
    nb = rows // BLK
    kb = blist.shape[1]
    tile = min(256, rows)
    me = lax.axis_index("row")
    sgn = 1 - 2 * lax.rem(me, 2)

    def dev(offset):
        return lax.rem(me + offset + n, n)

    source = [dev(sgn), dev(-2), dev(2), dev(-3 * sgn), dev(sgn - 2), dev(sgn + 2)]
    target = [dev(sgn), dev(2), dev(-2), dev(-3 * sgn), dev(sgn + 2), dev(sgn - 2)]

    barrier = pltpu.get_barrier_semaphore()
    for r in range(ROLES):
        pl.semaphore_signal(barrier, inc=1, device_id={"row": target[r]}, device_id_type=MESH)
    pl.semaphore_wait(barrier, ROLES)

    own_left = (s1, s2)
    own_right = (s2, s1)

    def direct(kind, role):
        return pltpu.make_async_remote_copy(
            src_ref=own_right[kind], dst_ref=win.at[kind, role],
            send_sem=send_sem.at[kind, role], recv_sem=recv_sem.at[kind, role],
            device_id={"row": target[role]}, device_id_type=MESH,
        )

    def forward(kind, role):
        return pltpu.make_async_remote_copy(
            src_ref=win.at[kind, role - 3], dst_ref=win.at[kind, role],
            send_sem=send_sem.at[kind, role], recv_sem=recv_sem.at[kind, role],
            device_id={"row": target[0]}, device_id_type=MESH,
        )

    def level_copy(kind, role):
        return pltpu.make_async_remote_copy(
            src_ref=levw.at[kind, OWN], dst_ref=levw.at[kind, role],
            send_sem=lev_send.at[kind, role], recv_sem=lev_recv.at[kind, role],
            device_id={"row": target[role]}, device_id_type=MESH,
        )

    for kind in range(2):
        for role in (3, 1, 2, 0):
            direct(kind, role).start()

    lane_block = lax.broadcasted_iota(jnp.int32, (1, rows), 1) // BLK
    for slot, owner in enumerate(source + [me]):
        footw[slot, 0:1, :] = foot[pl.ds(owner, 1), :]
        columns = lane_block + owner * nb
        for b in range(nb):
            hit = jnp.zeros((1, rows), jnp.float32)
            for k in range(kb):
                hit = jnp.where(columns == blist[me * nb + b, k], 1.0, hit)
            act[0, slot, b : b + 1, :] = hit
        hits = [jnp.zeros((1, rows), jnp.float32) for _ in range(nb)]
        for k in range(kb):
            listed = jnp.full((1, rows), blist[owner * nb, k], jnp.int32)
            for b in range(1, nb):
                listed = jnp.where(lane_block == b, blist[owner * nb + b, k], listed)
            for b in range(nb):
                hits[b] = jnp.where(listed == me * nb + b, 1.0, hits[b])
        for b in range(nb):
            act[1, slot, b : b + 1, :] = hits[b]
    footc[...] = jnp.transpose(jnp.broadcast_to(foot[pl.ds(me, 1), :], (BLK, rows)))
    mx[...] = jnp.full(mx.shape, NEGATIVE, jnp.float32)
    sm[...] = jnp.zeros(sm.shape, jnp.float32)
    eye = lax.broadcasted_iota(jnp.int32, (BLK, BLK), 0) == lax.broadcasted_iota(
        jnp.int32, (BLK, BLK), 1
    )

    def stats(kind, slot, right, diag):
        for t in range(rows // tile):
            raw = lax.dot_general(
                own_left[kind][t * tile : (t + 1) * tile, :], right,
                (((1,), (1,)), ((), ())), preferred_element_type=jnp.float32,
            )
            for u in range(tile // BLK):
                b = t * (tile // BLK) + u
                span = slice(b * BLK, (b + 1) * BLK)
                top = mx[kind, span, :]
                new = top
                parts = []
                for j in range(nb):
                    cols = slice(j * BLK, (j + 1) * BLK)
                    valid = footc[span, :] != footw[slot, 0:1, cols]
                    if diag and j == b:
                        valid = jnp.logical_or(valid, eye)
                    valid = jnp.logical_and(valid, act[kind, slot, b : b + 1, cols] > 0.0)
                    part = jnp.where(valid, raw[u * BLK : (u + 1) * BLK, cols], NEGATIVE)
                    logit[kind, slot, span, cols] = part
                    parts.append(part)
                    new = jnp.maximum(new, part)
                total = sm[kind, span, :] * jnp.exp(top - new)
                for part in parts:
                    total = total + jnp.exp(part - new)
                mx[kind, span, :] = new
                sm[kind, span, :] = total

    def levels(kind):
        top = mx[kind]
        highest = jnp.max(top, axis=1, keepdims=True)
        total = jnp.sum(sm[kind] * jnp.exp(top - highest), axis=1, keepdims=True)
        wide = jnp.broadcast_to(highest + jnp.log(total), (rows, BLK))
        levc[kind] = wide
        levw[kind, OWN] = jnp.transpose(wide)[0:8, :]
        for role in range(ROLES):
            level_copy(kind, role).start()

    for kind in range(2):
        stats(kind, OWN, own_right[kind][...], True)

    for kind in range(2):

        def arrive(role, carry, kind=kind):
            pltpu.make_async_copy(win.at[kind, role], win.at[kind, role], recv_sem.at[kind, role]).wait()

            @pl.when(jnp.logical_or(role == 1, role == 2))
            def _():
                pltpu.make_async_remote_copy(
                    src_ref=win.at[kind, role], dst_ref=win.at[kind, role + 3],
                    send_sem=send_sem.at[kind, role + 3], recv_sem=recv_sem.at[kind, role + 3],
                    device_id={"row": target[0]}, device_id_type=MESH,
                ).start()

            stats(kind, role, win[kind, role], False)
            return carry

        lax.fori_loop(0, ROLES, arrive, 0)
        levels(kind)

    def grads(kind, slot, right, out, diag):
        for t in range(rows // tile):
            pieces = []
            for u in range(tile // BLK):
                b = t * (tile // BLK) + u
                span = slice(b * BLK, (b + 1) * BLK)
                mine = levc[kind, span, :]
                across = []
                for j in range(nb):
                    cols = slice(j * BLK, (j + 1) * BLK)
                    part = logit[kind, slot, span, cols]
                    weight = 0.5 * (
                        jnp.exp(part - mine) + jnp.exp(part - levw[1 - kind, slot, 0:1, cols])
                    )
                    if diag and j == b:
                        weight = weight - jnp.where(eye, 1.0, 0.0)
                    across.append(weight.astype(jnp.bfloat16))
                pieces.append(jnp.concatenate(across, axis=1))
            weights = jnp.concatenate(pieces, axis=0)
            part = jnp.dot(weights, right, preferred_element_type=jnp.float32)
            span = slice(t * tile, (t + 1) * tile)
            if diag:
                out[span, :] = part
            else:
                out[span, :] = out[span, :] + part

    outs = (g1, g2)
    for kind in (1, 0):
        grads(kind, OWN, own_right[kind][...], outs[kind], True)

        def step(role, carry, kind=kind):
            other = levw.at[1 - kind, role]
            pltpu.make_async_copy(other, other, lev_recv.at[1 - kind, role]).wait()
            grads(kind, role, win[kind, role], outs[kind], False)
            return carry

        lax.fori_loop(0, ROLES, step, 0)

    for kind in range(2):
        for role in range(4):
            direct(kind, role).wait_send()
        for role in range(4, 6):
            forward(kind, role).wait_send()
        for role in range(ROLES):
            level_copy(kind, role).wait_send()


def shards(s1_embed, s2_embed, block_list, footprint):
    rows, width = s1_embed.shape
    n = lax.axis_size("row")
    foot = footprint.astype(jnp.float32).reshape(n, rows)
    vmem = pl.BlockSpec(memory_space=pltpu.VMEM)
    return pl.pallas_call(
        functools.partial(kernel, n),
        out_shape=(
            jax.ShapeDtypeStruct((rows, width), jnp.float32),
            jax.ShapeDtypeStruct((rows, width), jnp.float32),
        ),
        in_specs=[vmem, vmem, pl.BlockSpec(memory_space=pltpu.SMEM), vmem],
        out_specs=(vmem, vmem),
        scratch_shapes=[
            pltpu.VMEM((2, ROLES, rows, width), jnp.bfloat16),
            pltpu.VMEM((2, ROLES + 1, rows, rows), jnp.float32),
            pltpu.VMEM((2, ROLES + 1, 8, rows), jnp.float32),
            pltpu.VMEM((ROLES + 1, 8, rows), jnp.float32),
            pltpu.VMEM((rows, BLK), jnp.float32),
            pltpu.VMEM((2, rows, BLK), jnp.float32),
            pltpu.VMEM((2, rows, BLK), jnp.float32),
            pltpu.VMEM((2, rows, BLK), jnp.float32),
            pltpu.VMEM((2, ROLES + 1, 8, rows), jnp.float32),
            pltpu.SemaphoreType.DMA((2, ROLES)),
            pltpu.SemaphoreType.DMA((2, ROLES)),
            pltpu.SemaphoreType.DMA((2, ROLES)),
            pltpu.SemaphoreType.DMA((2, ROLES)),
        ],
        compiler_params=pltpu.CompilerParams(
            collective_id=0, has_side_effects=True, vmem_limit_bytes=52 * 1024 * 1024
        ),
    )(s1_embed, s2_embed, block_list, foot)


def solution(mesh):
    placed = (P(("grp", "row"), None), P(("grp", "row"), None), P("grp", None), P("grp"))
    return jax.shard_map(
        shards,
        mesh=mesh,
        in_specs=placed,
        out_specs=(P(("grp", "row"), None), P(("grp", "row"), None)),
        check_vma=False,
    )
```

time: 284 us -> 100 us (0.35)
  waiting for transfers between devices: 133 us -> 0 us
  Pallas kernels: 0 us -> 91.5 us
  matrix products: 55.4 us -> 0 us
  starting transfers between devices: 45.1 us -> 0 us
  other arithmetic: 29.3 us -> 0.76 us
  local copies, waits for them, and re-layouts: 15.1 us -> 6.96 us
  between operations: 5.33 us -> 0.66 us
    ppermute x30 -> x0, waiting for transfers between devices: 133 us -> none  [passed_along(): lax.ppermute(array, axis, [(i, (i + by) % count) for i in range(count)])]
    pallas_call x0 -> x1, Pallas kernels: none -> 91.5 us  [shards(): pl.pallas_call(functools.partial(kernel, n), out_shape=(jax.ShapeDtypeStr...]
    dot_general x28 -> x0, matrix products: 55.4 us -> none  [the longest x14 32.1 us: pair_scores(): lax.dot_general(row_embed, column_embed, (((1,), (1,)), ((), ())), prefer...]
    ppermute x30 -> x0, starting transfers between devices: 45.1 us -> none  [passed_along(): lax.ppermute(array, axis, [(i, (i + by) % count) for i in range(count)])]
    add x8 -> x0, other arithmetic: 13.1 us -> none  [the longest x1 6.01 us: shards(): grad_s2 = grad_s2 + passed_along(to_columns, 'row', offset)]
    broadcast_in_dim x14 -> x0, local copies, waits for them, and re-layouts: 11.3 us -> none  [slot_mask(): spread = jnp.repeat(jnp.repeat(active, BLK, axis=0), BLK, axis=1)]
    reduce_sum x7 -> x0, other arithmetic: 8.7 us -> none  [work(): jnp.sum(jnp.where(valid, jnp.exp(masked - column_top[None, :]), 0.0), axi...]
    and x9 -> x0, other arithmetic: 6.64 us -> none  [the longest x7 4.17 us: slot_mask(): jnp.logical_and(row_device == column_device, jnp.eye(rows, dtype=jnp.bool_))]
  transfers between devices with their start and end apart: 30 -> 0, of which waited for: 5 -> 0; matrix products, arithmetic and copies ran while one was open for 30% -> 0% of each run, Pallas kernels for 0% -> 0%
where the time goes in v1:
time: 100 us; the launch traced here: 99.8 us
  Pallas kernels  91.5 us (92%)
  local copies, waits for them, and re-layouts  6.96 us (7%)
    pallas_call x1, Pallas kernels, shards(): pl.pallas_call(functools.partial(kernel, n), out_shape=(jax.ShapeDtypeStr...  91.5 us
    unnamed x9, local copies, waits for them, and re-layouts  6.95 us

profile of v1, /device:TPU:1, one launch (start us, length us, event | category | flops | bytes accessed | tf_op | source)
XLA Modules:
  0.0 99.8 jit_solution(3792793236001733003)
XLA Ops:
  0.6 0.8 copy.6.blist
  1.4 0.8 convert_element_type.3
  2.2 0.0 copy-start
  2.2 1.1 %copy-done = bf16[512,768]{1,0:T(8,128)(2,1)S(1)} copy-done((bf16[512,768]{1,0:T(8,128)(2,1)S(1)}, bf16[512,768]{1,0:T(8,128)(2,1)}, u32[]{:S(2)}) %copy-start) | copy-done | bytes 786456
  3.3 0.0 copy-start.1
  3.3 1.1 %copy-done.1 = bf16[512,768]{1,0:T(8,128)(2,1)S(1)} copy-done((bf16[512,768]{1,0:T(8,128)(2,1)S(1)}, bf16[512,768]{1,0:T(8,128)(2,1)}, u32[]{:S(2)}) %copy-start.1) | copy-done | bytes 786456
  4.4 91.5 %shard_map.59 = (f32[512,768]{1,0:T(8,128)}, f32[512,768]{1,0:T(8,128)}) custom-call(bf16[512,768]{1,0:T(8,128)(2,1)S(1)} %copy-done, bf16[512,768]{1,0:T(8,128)(2,1)S(1)} %copy-done.1, s32[64,4]{1,0:T(8,128)S(1)} %copy.6.blist, f32[16,512]{1,0:T(8,128)S(1)} %reshape.7.foot), custom_call_target="tpu_custom_call" | custom-call | tf_op jit(solution)/shard_map/pallas_call | solution.py:205
  95.9 0.0 copy-start.2
  95.9 2.8 %copy.9 = f32[512,768]{1,0:T(8,128)} copy(f32[512,768]{1,0:T(8,128)} %get-tuple-element.4) | data formatting | bytes 3145728
  98.7 0.0 copy-done.2
  98.7 1.1 %copy.10 = f32[512,768]{1,0:T(8,128)} copy(f32[512,768]{1,0:T(8,128)S(1)} %copy-done.2) | data formatting | bytes 3145728
  (1 shorter events, 0.0 us)
Async XLA Ops:
  2.2 1.1 %copy-start = (bf16[512,768]{1,0:T(8,128)(2,1)S(1)}, bf16[512,768]{1,0:T(8,128)(2,1)}, u32[]{:S(2)}) copy-start(bf16[512,768]{1,0:T(8,128)(2,1)} %s1_.1) | copy-start | bytes 2359300
  3.3 1.1 %copy-start.1 = (bf16[512,768]{1,0:T(8,128)(2,1)S(1)}, bf16[512,768]{1,0:T(8,128)(2,1)}, u32[]{:S(2)}) copy-start(bf16[512,768]{1,0:T(8,128)(2,1)} %s2_.1) | copy-start | bytes 2359300
  95.9 2.8 %copy-start.2 = (f32[512,768]{1,0:T(8,128)S(1)}, f32[512,768]{1,0:T(8,128)}, u32[]{:S(2)}) copy-start(f32[512,768]{1,0:T(8,128)} %get-tuple-element.5) | copy-start | bytes 4718596

commit v2 on v1

--- a/solution.py
+++ b/solution.py
@@ -24,18 +24,32 @@
     kb = blist.shape[1]
     tile = min(256, rows)
     me = lax.axis_index("row")
-    sgn = 1 - 2 * lax.rem(me, 2)
+    core = lax.rem(me, 2)
+    chip = me // 2
+    side = lax.rem(chip, 2)
+    sgn = 1 - 2 * core
+    sy = 1 - 2 * side
+    odd = lax.rem(core + side, 2)
 
     def dev(offset):
         return lax.rem(me + offset + n, n)
 
-    source = [dev(sgn), dev(-2), dev(2), dev(-3 * sgn), dev(sgn - 2), dev(sgn + 2)]
-    target = [dev(sgn), dev(2), dev(-2), dev(-3 * sgn), dev(sgn + 2), dev(sgn - 2)]
+    def at_chip(offset, which):
+        return lax.rem(2 * (chip + offset) + which + n, n)
+
+    partner, across, straight = dev(sgn), dev(2 * sy), dev(-3 * sgn)
+    source = [
+        partner, across, straight, dev(2 * sy + sgn), at_chip(-sy, 1 - side), at_chip(-sy, side)
+    ]
+    target = [partner, across, straight, dev(2 * sy + sgn), at_chip(-sy, 0), at_chip(-sy, 1)]
+    landing = [0, 1, 2, 3, 4 + odd, 4 + odd]
+    relay_to = dev(sy * (5 - 3 * odd))
+    relay_peer = dev(sy * (5 - 10 * odd))
 
     barrier = pltpu.get_barrier_semaphore()
-    for r in range(ROLES):
-        pl.semaphore_signal(barrier, inc=1, device_id={"row": target[r]}, device_id_type=MESH)
-    pl.semaphore_wait(barrier, ROLES)
+    for peer in target + [relay_peer]:
+        pl.semaphore_signal(barrier, inc=1, device_id={"row": peer}, device_id_type=MESH)
+    pl.semaphore_wait(barrier, ROLES + 1)
 
     own_left = (s1, s2)
     own_right = (s2, s1)
@@ -47,22 +61,31 @@
             device_id={"row": target[role]}, device_id_type=MESH,
         )
 
-    def forward(kind, role):
+    def passed(kind, held, slot, sem, to):
         return pltpu.make_async_remote_copy(
-            src_ref=win.at[kind, role - 3], dst_ref=win.at[kind, role],
-            send_sem=send_sem.at[kind, role], recv_sem=recv_sem.at[kind, role],
-            device_id={"row": target[0]}, device_id_type=MESH,
+            src_ref=win.at[kind, held], dst_ref=win.at[kind, slot],
+            send_sem=send_sem.at[kind, sem], recv_sem=recv_sem.at[kind, slot],
+            device_id={"row": to}, device_id_type=MESH,
         )
+
+    def hand_over(kind):
+        return passed(kind, 1, 3, 3, partner)
+
+    def relay(kind):
+        return passed(kind, 1 + odd, 5 - odd, 4, relay_to)
+
+    def share(kind):
+        return passed(kind, 4 + odd, 4 + odd, 5, partner)
 
     def level_copy(kind, role):
         return pltpu.make_async_remote_copy(
-            src_ref=levw.at[kind, OWN], dst_ref=levw.at[kind, role],
-            send_sem=lev_send.at[kind, role], recv_sem=lev_recv.at[kind, role],
+            src_ref=levw.at[kind, OWN], dst_ref=levw.at[kind, landing[role]],
+            send_sem=lev_send.at[kind, role], recv_sem=lev_recv.at[kind, landing[role]],
             device_id={"row": target[role]}, device_id_type=MESH,
         )
 
     for kind in range(2):
-        for role in (3, 1, 2, 0):
+        for role in (2, 1, 0):
             direct(kind, role).start()
 
     lane_block = lax.broadcasted_iota(jnp.int32, (1, rows), 1) // BLK
@@ -131,23 +154,42 @@
     for kind in range(2):
         stats(kind, OWN, own_right[kind][...], True)
 
-    for kind in range(2):
-
-        def arrive(role, carry, kind=kind):
-            pltpu.make_async_copy(win.at[kind, role], win.at[kind, role], recv_sem.at[kind, role]).wait()
-
-            @pl.when(jnp.logical_or(role == 1, role == 2))
+    def landed(kind, slot):
+        block = win.at[kind, slot]
+        pltpu.make_async_copy(block, block, recv_sem.at[kind, slot]).wait()
+
+    for kind in range(2):
+
+        def near(slot, carry, kind=kind):
+            landed(kind, slot)
+
+            @pl.when(slot == 1)
             def _():
-                pltpu.make_async_remote_copy(
-                    src_ref=win.at[kind, role], dst_ref=win.at[kind, role + 3],
-                    send_sem=send_sem.at[kind, role + 3], recv_sem=recv_sem.at[kind, role + 3],
-                    device_id={"row": target[0]}, device_id_type=MESH,
-                ).start()
-
-            stats(kind, role, win[kind, role], False)
+                hand_over(kind).start()
+
+            @pl.when(slot == 1 + odd)
+            def _():
+                relay(kind).start()
+
+            stats(kind, slot, win[kind, slot], False)
             return carry
 
-        lax.fori_loop(0, ROLES, arrive, 0)
+        lax.fori_loop(0, 4, near, 0)
+
+    for kind in range(2):
+
+        def far(j, carry, kind=kind):
+            slot = 4 + lax.rem(odd + j, 2)
+            landed(kind, slot)
+
+            @pl.when(j == 0)
+            def _():
+                share(kind).start()
+
+            stats(kind, slot, win[kind, slot], False)
+            return carry
+
+        lax.fori_loop(0, 2, far, 0)
         levels(kind)
 
     def grads(kind, slot, right, out, diag):
@@ -189,10 +231,11 @@
         lax.fori_loop(0, ROLES, step, 0)
 
     for kind in range(2):
-        for role in range(4):
+        for role in range(3):
             direct(kind, role).wait_send()
-        for role in range(4, 6):
-            forward(kind, role).wait_send()
+        hand_over(kind).wait_send()
+        relay(kind).wait_send()
+        share(kind).wait_send()
         for role in range(ROLES):
             level_copy(kind, role).wait_send()
 

time: 100 us -> 82.3 us (0.82)
  Pallas kernels: 91.5 us -> 73.6 us
    pallas_call x1, Pallas kernels: 91.5 us -> 73.6 us  [shards(): pl.pallas_call(functools.partial(kernel, n), out_shape=(jax.ShapeDtypeStr...]
where the time goes in v2:
time: 82.3 us; the launch traced here: 82 us
  Pallas kernels  73.6 us (89%)
  local copies, waits for them, and re-layouts  6.96 us (8%)
    pallas_call x1, Pallas kernels, shards(): pl.pallas_call(functools.partial(kernel, n), out_shape=(jax.ShapeDtypeStr...  73.6 us
    unnamed x9, local copies, waits for them, and re-layouts  6.95 us

profile of v2, /device:TPU:1, one launch (start us, length us, event | category | flops | bytes accessed | tf_op | source)
XLA Modules:
  0.0 82.0 jit_solution(6614283705021812056)
XLA Ops:
  0.6 0.8 copy.6.blist
  1.4 0.8 convert_element_type.3
  2.2 0.0 copy-start
  2.2 1.1 %copy-done = bf16[512,768]{1,0:T(8,128)(2,1)S(1)} copy-done((bf16[512,768]{1,0:T(8,128)(2,1)S(1)}, bf16[512,768]{1,0:T(8,128)(2,1)}, u32[]{:S(2)}) %copy-start) | copy-done | bytes 786456
  3.3 0.0 copy-start.1
  3.3 1.1 %copy-done.1 = bf16[512,768]{1,0:T(8,128)(2,1)S(1)} copy-done((bf16[512,768]{1,0:T(8,128)(2,1)S(1)}, bf16[512,768]{1,0:T(8,128)(2,1)}, u32[]{:S(2)}) %copy-start.1) | copy-done | bytes 786456
  4.4 73.6 %shard_map.59 = (f32[512,768]{1,0:T(8,128)}, f32[512,768]{1,0:T(8,128)}) custom-call(bf16[512,768]{1,0:T(8,128)(2,1)S(1)} %copy-done, bf16[512,768]{1,0:T(8,128)(2,1)S(1)} %copy-done.1, s32[64,4]{1,0:T(8,128)S(1)} %copy.6.blist, f32[16,512]{1,0:T(8,128)S(1)} %reshape.7.foot), custom_call_target="tpu_custom_call" | custom-call | tf_op jit(solution)/shard_map/pallas_call | solution.py:248
  78.1 0.0 copy-start.2
  78.1 2.8 %copy.9 = f32[512,768]{1,0:T(8,128)} copy(f32[512,768]{1,0:T(8,128)} %get-tuple-element.4) | data formatting | bytes 3145728
  80.9 0.0 copy-done.2
  80.9 1.1 %copy.10 = f32[512,768]{1,0:T(8,128)} copy(f32[512,768]{1,0:T(8,128)S(1)} %copy-done.2) | data formatting | bytes 3145728
  (1 shorter events, 0.0 us)
Async XLA Ops:
  2.2 1.1 %copy-start = (bf16[512,768]{1,0:T(8,128)(2,1)S(1)}, bf16[512,768]{1,0:T(8,128)(2,1)}, u32[]{:S(2)}) copy-start(bf16[512,768]{1,0:T(8,128)(2,1)} %s1_.1) | copy-start | bytes 2359300
  3.3 1.1 %copy-start.1 = (bf16[512,768]{1,0:T(8,128)(2,1)S(1)}, bf16[512,768]{1,0:T(8,128)(2,1)}, u32[]{:S(2)}) copy-start(bf16[512,768]{1,0:T(8,128)(2,1)} %s2_.1) | copy-start | bytes 2359300
  78.1 2.8 %copy-start.2 = (f32[512,768]{1,0:T(8,128)S(1)}, f32[512,768]{1,0:T(8,128)}, u32[]{:S(2)}) copy-start(f32[512,768]{1,0:T(8,128)} %get-tuple-element.5) | copy-start | bytes 4718596

commit v3 on v2

--- a/solution.py
+++ b/solution.py
@@ -15,13 +15,13 @@
 
 
 def kernel(
-    n, s1, s2, blist, foot, g1, g2,
-    win, logit, act, footw, footc, mx, sm, levc, levw,
+    n, s1, s2, blist, foot_all, g1, g2,
+    own, foot, load_sem, win, logit, act, footw, footc, mx, sm, levc, levw,
     send_sem, recv_sem, lev_send, lev_recv,
 ):
     rows, width = s1.shape
     nb = rows // BLK
-    kb = blist.shape[1]
+    kb = blist.shape[0]
     tile = min(256, rows)
     me = lax.axis_index("row")
     core = lax.rem(me, 2)
@@ -51,7 +51,6 @@
         pl.semaphore_signal(barrier, inc=1, device_id={"row": peer}, device_id_type=MESH)
     pl.semaphore_wait(barrier, ROLES + 1)
 
-    own_left = (s1, s2)
     own_right = (s2, s1)
 
     def direct(kind, role):
@@ -88,25 +87,37 @@
         for role in (2, 1, 0):
             direct(kind, role).start()
 
+    loads = [
+        pltpu.make_async_copy(foot_all, foot, load_sem.at[2]),
+        pltpu.make_async_copy(s1, own.at[0], load_sem.at[0]),
+        pltpu.make_async_copy(s2, own.at[1], load_sem.at[1]),
+    ]
+    for load in loads:
+        load.start()
+    loads[0].wait()
+
     lane_block = lax.broadcasted_iota(jnp.int32, (1, rows), 1) // BLK
     for slot, owner in enumerate(source + [me]):
-        footw[slot, 0:1, :] = foot[pl.ds(owner, 1), :]
+        for b in range(nb):
+            footw[slot, 0:1, b * BLK : (b + 1) * BLK] = foot[pl.ds(owner * nb + b, 1), :].astype(
+                jnp.float32
+            )
         columns = lane_block + owner * nb
         for b in range(nb):
             hit = jnp.zeros((1, rows), jnp.float32)
             for k in range(kb):
-                hit = jnp.where(columns == blist[me * nb + b, k], 1.0, hit)
+                hit = jnp.where(columns == blist[k, me * nb + b], 1.0, hit)
             act[0, slot, b : b + 1, :] = hit
         hits = [jnp.zeros((1, rows), jnp.float32) for _ in range(nb)]
         for k in range(kb):
-            listed = jnp.full((1, rows), blist[owner * nb, k], jnp.int32)
+            listed = jnp.full((1, rows), blist[k, owner * nb], jnp.int32)
             for b in range(1, nb):
-                listed = jnp.where(lane_block == b, blist[owner * nb + b, k], listed)
+                listed = jnp.where(lane_block == b, blist[k, owner * nb + b], listed)
             for b in range(nb):
                 hits[b] = jnp.where(listed == me * nb + b, 1.0, hits[b])
         for b in range(nb):
             act[1, slot, b : b + 1, :] = hits[b]
-    footc[...] = jnp.transpose(jnp.broadcast_to(foot[pl.ds(me, 1), :], (BLK, rows)))
+    footc[...] = jnp.transpose(jnp.broadcast_to(footw[OWN, 0:1, :], (BLK, rows)))
     mx[...] = jnp.full(mx.shape, NEGATIVE, jnp.float32)
     sm[...] = jnp.zeros(sm.shape, jnp.float32)
     eye = lax.broadcasted_iota(jnp.int32, (BLK, BLK), 0) == lax.broadcasted_iota(
@@ -116,7 +127,7 @@
     def stats(kind, slot, right, diag):
         for t in range(rows // tile):
             raw = lax.dot_general(
-                own_left[kind][t * tile : (t + 1) * tile, :], right,
+                own[kind, t * tile : (t + 1) * tile, :], right,
                 (((1,), (1,)), ((), ())), preferred_element_type=jnp.float32,
             )
             for u in range(tile // BLK):
@@ -151,8 +162,10 @@
         for role in range(ROLES):
             level_copy(kind, role).start()
 
-    for kind in range(2):
-        stats(kind, OWN, own_right[kind][...], True)
+    loads[1].wait()
+    loads[2].wait()
+    for kind in range(2):
+        stats(kind, OWN, own[1 - kind], True)
 
     def landed(kind, slot):
         block = win.at[kind, slot]
@@ -220,7 +233,7 @@
 
     outs = (g1, g2)
     for kind in (1, 0):
-        grads(kind, OWN, own_right[kind][...], outs[kind], True)
+        grads(kind, OWN, own[1 - kind], outs[kind], True)
 
         def step(role, carry, kind=kind):
             other = levw.at[1 - kind, role]
@@ -243,17 +256,21 @@
 def shards(s1_embed, s2_embed, block_list, footprint):
     rows, width = s1_embed.shape
     n = lax.axis_size("row")
-    foot = footprint.astype(jnp.float32).reshape(n, rows)
+    foot = footprint.reshape(n * (rows // BLK), BLK)
     vmem = pl.BlockSpec(memory_space=pltpu.VMEM)
+    hbm = pl.BlockSpec(memory_space=pltpu.HBM)
     return pl.pallas_call(
         functools.partial(kernel, n),
         out_shape=(
             jax.ShapeDtypeStruct((rows, width), jnp.float32),
             jax.ShapeDtypeStruct((rows, width), jnp.float32),
         ),
-        in_specs=[vmem, vmem, pl.BlockSpec(memory_space=pltpu.SMEM), vmem],
+        in_specs=[hbm, hbm, pl.BlockSpec(memory_space=pltpu.SMEM), hbm],
         out_specs=(vmem, vmem),
         scratch_shapes=[
+            pltpu.VMEM((2, rows, width), jnp.bfloat16),
+            pltpu.VMEM(foot.shape, jnp.int32),
+            pltpu.SemaphoreType.DMA((3,)),
             pltpu.VMEM((2, ROLES, rows, width), jnp.bfloat16),
             pltpu.VMEM((2, ROLES + 1, rows, rows), jnp.float32),
             pltpu.VMEM((2, ROLES + 1, 8, rows), jnp.float32),
@@ -269,9 +286,9 @@
             pltpu.SemaphoreType.DMA((2, ROLES)),
         ],
         compiler_params=pltpu.CompilerParams(
-            collective_id=0, has_side_effects=True, vmem_limit_bytes=52 * 1024 * 1024
+            collective_id=0, has_side_effects=True, vmem_limit_bytes=63 * 1024 * 1024
         ),
-    )(s1_embed, s2_embed, block_list, foot)
+    )(s1_embed, s2_embed, block_list.T, foot)
 
 
 def solution(mesh):

time: 82.3 us -> 78.3 us (0.951)
  local copies, waits for them, and re-layouts: 6.96 us -> 3.92 us
    unnamed x9 -> x4, local copies, waits for them, and re-layouts: 6.95 us -> 3.92 us
where the time goes in v3:
time: 78.3 us; the launch traced here: 78.1 us
  Pallas kernels  73.5 us (94%)
  local copies, waits for them, and re-layouts  3.92 us (5%)
    pallas_call x1, Pallas kernels, shards(): pl.pallas_call(functools.partial(kernel, n), out_shape=(jax.ShapeDtypeStr...  73.5 us
    unnamed x4, local copies, waits for them, and re-layouts  3.92 us

profile of v3, /device:TPU:1, one launch (start us, length us, event | category | flops | bytes accessed | tf_op | source)
XLA Modules:
  0.0 78.1 jit_solution(2802863728131793586)
XLA Ops:
  0.6 73.5 %shard_map.59 = (f32[512,768]{1,0:T(8,128)}, f32[512,768]{1,0:T(8,128)}) custom-call(bf16[512,768]{1,0:T(8,128)(2,1)} %s1_.1, bf16[512,768]{1,0:T(8,128)(2,1)} %s2_.1, s32[4,64]{1,0:T(4,128)} %bitcast.3, s32[64,128]{1,0:T(8,128)} %bitcast.2), custom_call_target="tpu_custom_call" | custom-call | tf_op jit(solution)/shard_map/pallas_call | solution.py:262
  74.2 0.0 copy-start
  74.2 2.8 %copy.8 = f32[512,768]{1,0:T(8,128)} copy(f32[512,768]{1,0:T(8,128)} %get-tuple-element.4) | data formatting | bytes 3145728
  77.0 0.0 copy-done
  77.0 1.1 %copy.9 = f32[512,768]{1,0:T(8,128)} copy(f32[512,768]{1,0:T(8,128)S(1)} %copy-done) | data formatting | bytes 3145728
Async XLA Ops:
  74.2 2.8 %copy-start = (f32[512,768]{1,0:T(8,128)S(1)}, f32[512,768]{1,0:T(8,128)}, u32[]{:S(2)}) copy-start(f32[512,768]{1,0:T(8,128)} %get-tuple-element.5) | copy-start | bytes 4718596

commit v4 on v3

--- a/solution.py
+++ b/solution.py
@@ -10,13 +10,14 @@
 BLK = 128
 NEGATIVE = -1e30
 ROLES = 6
+PARTS = 4
 OWN = 6
 MESH = pl.DeviceIdType.MESH
 
 
 def kernel(
-    n, s1, s2, blist, foot_all, g1, g2,
-    own, foot, load_sem, win, logit, act, footw, footc, mx, sm, levc, levw,
+    n, s1, s2, blist, foot_all, g1_out, g2_out,
+    g1, g2, store_sem, own, foot, load_sem, win, logit, act, footw, footc, mx, sm, levc, levw,
     send_sem, recv_sem, lev_send, lev_recv,
 ):
     rows, width = s1.shape
@@ -232,6 +233,10 @@
                 out[span, :] = out[span, :] + part
 
     outs = (g1, g2)
+    stores = [
+        pltpu.make_async_copy(g1, g1_out, store_sem.at[0]),
+        pltpu.make_async_copy(g2, g2_out, store_sem.at[1]),
+    ]
     for kind in (1, 0):
         grads(kind, OWN, own[1 - kind], outs[kind], True)
 
@@ -242,6 +247,7 @@
             return carry
 
         lax.fori_loop(0, ROLES, step, 0)
+        stores[kind].start()
 
     for kind in range(2):
         for role in range(3):
@@ -251,23 +257,49 @@
         share(kind).wait_send()
         for role in range(ROLES):
             level_copy(kind, role).wait_send()
+        stores[kind].wait()
+
+
+def hand_out(a, b, a_out, b_out, held, in_sem, out_sem):
+    size = a.shape[0] // PARTS
+
+    def fetch(i, p):
+        span = pl.ds(p * size, size)
+        return pltpu.make_async_copy((a, b)[i].at[span, :], held.at[i, span, :], in_sem.at[i, p])
+
+    def store(i, p):
+        span = pl.ds(p * size, size)
+        return pltpu.make_async_copy(
+            held.at[i, span, :], (a_out, b_out)[i].at[span, :], out_sem.at[i, p]
+        )
+
+    order = [(i, p) for p in range(PARTS) for i in range(2)]
+    for i, p in order:
+        fetch(i, p).start()
+    for i, p in order:
+        fetch(i, p).wait()
+        store(i, p).start()
+    for i, p in order:
+        store(i, p).wait()
 
 
 def shards(s1_embed, s2_embed, block_list, footprint):
     rows, width = s1_embed.shape
     n = lax.axis_size("row")
     foot = footprint.reshape(n * (rows // BLK), BLK)
-    vmem = pl.BlockSpec(memory_space=pltpu.VMEM)
     hbm = pl.BlockSpec(memory_space=pltpu.HBM)
-    return pl.pallas_call(
+    made = pl.pallas_call(
         functools.partial(kernel, n),
         out_shape=(
             jax.ShapeDtypeStruct((rows, width), jnp.float32),
             jax.ShapeDtypeStruct((rows, width), jnp.float32),
         ),
         in_specs=[hbm, hbm, pl.BlockSpec(memory_space=pltpu.SMEM), hbm],
-        out_specs=(vmem, vmem),
+        out_specs=(hbm, hbm),
         scratch_shapes=[
+            pltpu.VMEM((rows, width), jnp.float32),
+            pltpu.VMEM((rows, width), jnp.float32),
+            pltpu.SemaphoreType.DMA((2,)),
             pltpu.VMEM((2, rows, width), jnp.bfloat16),
             pltpu.VMEM(foot.shape, jnp.int32),
             pltpu.SemaphoreType.DMA((3,)),
@@ -289,6 +321,21 @@
             collective_id=0, has_side_effects=True, vmem_limit_bytes=63 * 1024 * 1024
         ),
     )(s1_embed, s2_embed, block_list.T, foot)
+    return pl.pallas_call(
+        hand_out,
+        out_shape=(
+            jax.ShapeDtypeStruct((rows, width), jnp.float32),
+            jax.ShapeDtypeStruct((rows, width), jnp.float32),
+        ),
+        in_specs=[hbm, hbm],
+        out_specs=(hbm, hbm),
+        scratch_shapes=[
+            pltpu.VMEM((2, rows, width), jnp.float32),
+            pltpu.SemaphoreType.DMA((2, PARTS)),
+            pltpu.SemaphoreType.DMA((2, PARTS)),
+        ],
+        compiler_params=pltpu.CompilerParams(vmem_limit_bytes=63 * 1024 * 1024),
+    )(*made)
 
 
 def solution(mesh):

time: 78.3 us -> 76.7 us (0.980)
  local copies, waits for them, and re-layouts: 3.92 us -> 0 us
  Pallas kernels: 73.5 us -> 75.8 us
    unnamed x4 -> x0, local copies, waits for them, and re-layouts: 3.92 us -> none
    pallas_call x0 -> x1, Pallas kernels: none -> 2.79 us  [shards(): pl.pallas_call(hand_out, out_shape=(jax.ShapeDtypeStruct((rows, width), j...]
where the time goes in v4:
time: 76.7 us; the launch traced here: 76.5 us
  Pallas kernels  75.8 us (99%)
    pallas_call x1, Pallas kernels, shards(): pl.pallas_call(functools.partial(kernel, n), out_shape=(jax.ShapeDtypeStr...  73 us
    pallas_call x1, Pallas kernels, shards(): pl.pallas_call(hand_out, out_shape=(jax.ShapeDtypeStruct((rows, width), j...  2.79 us

profile of v4, /device:TPU:1, one launch (start us, length us, event | category | flops | bytes accessed | tf_op | source)
XLA Modules:
  0.0 76.5 jit_solution(15242848836874066387)
XLA Ops:
  0.6 73.0 %shard_map.59 = (f32[512,768]{1,0:T(8,128)}, f32[512,768]{1,0:T(8,128)}) custom-call(bf16[512,768]{1,0:T(8,128)(2,1)} %s1_.1, bf16[512,768]{1,0:T(8,128)(2,1)} %s2_.1, s32[4,64]{1,0:T(4,128)} %bitcast.3, s32[64,128]{1,0:T(8,128)} %bitcast.2), custom_call_target="tpu_custom_call" | custom-call | tf_op jit(solution)/shard_map/pallas_call | solution.py:291
  73.7 2.8 %shard_map.60 = (f32[512,768]{1,0:T(8,128)}, f32[512,768]{1,0:T(8,128)}) custom-call(f32[512,768]{1,0:T(8,128)} %get-tuple-element.4.a, f32[512,768]{1,0:T(8,128)} %get-tuple-element.5.b), custom_call_target="tpu_custom_call" | custom-call | tf_op jit(solution)/shard_map/pallas_call | solution.py:324
